TPU v7x, 32 devices: a whole 2x2x4 slice. The times are simulated.
32 devices in a mesh: pair: 8 (over z, y), grid: 4 (over x, core).
Axes of the slice: x: 2, y: 2, z: 4, core: 2. Of those that a mesh axis runs over, the one named last changes fastest.
Arguments:
- adjoint: bfloat16 [2048, 9, 2001], P(('pair', 'grid')), may hold values from -0.29882812 to 0.29882812
- first_block: int32 [2048, 1], P(('pair', 'grid')), may hold values from 0 to 31; in each aligned block of 64 rows (0 to 63, 64 to 127, ...) at most 3 rows name the same one
- second_station: int32 [2048], P(('pair', 'grid')), may hold values from 0 to 3999
- station_block: int32 [4000], replicated, may hold values from 0 to 31
- lag_lo: int32 [2048], P(('pair', 'grid')), may hold values from 0 to 999
- lag_hi: int32 [2048], P(('pair', 'grid')), may hold values from 1001 to 2001
- pair_count: int32 [32], P(('pair', 'grid')), may hold values from 1 to 64, 1536 in all
- green_function: bfloat16 [32, 3, 2, 512, 2048], P(None, None, None, 'pair', 'grid'), may hold values from -0.11 to 0.11
Outputs:
- kernel: float32 [2, 2048], P(None, 'grid')
Inputs may be any that keep to these rules, and one draw needn't show every extreme that they name: `first_block`: in the rows of one device no block is named by more than 3 rows. Slots 0 to pair_count - 1 of a device hold live pairs, the others padding.
All inputs are finite; a program needn't handle non-finite values.
Results may differ from a plain program's by a relative error of at most 0.0047.
Values may be sent and summed in bfloat16 or wider, within the bound.
A program may use at most 128 MiB of HBM per device.

v0:
```python
import math

import jax
import jax.numpy as jnp
from jax import lax
from jax.sharding import PartitionSpec as P

NF = 256
BANDS = 2


def dft_table(lag_count, freq_count, band_width):
    offsets = jnp.arange(lag_count, dtype=jnp.int32) - lag_count // 2
    indices = jnp.arange(freq_count, dtype=jnp.int32)
    freq_bins = 24 + indices + 64 * (indices // band_width)
    phases = jnp.mod(offsets[:, None] * freq_bins[None, :], lag_count).astype(jnp.float32) * (
        2.0 * math.pi / lag_count
    )
    return jnp.concatenate([jnp.cos(phases), -jnp.sin(phases)], axis=1).astype(jnp.bfloat16)


def transform_rows(signal, phase_table):
    lag_count = signal.shape[-1]
    flat = signal.reshape(-1, lag_count)
    result = jnp.dot(flat, phase_table, preferred_element_type=jnp.float32).astype(jnp.bfloat16)
    return result.reshape(signal.shape[:-1] + (phase_table.shape[1],))


def contract(field, factor):
    return jnp.einsum("vbfx,uvabf->uafx", field, factor, preferred_element_type=jnp.float32)


def body(
    adjoint, first_block, second_station, station_block, lag_lo, lag_hi, pair_count, green_function
):
    row_count, comp_count, lag_count = adjoint.shape
    block_count = green_function.shape[0]
    local_freqs = green_function.shape[3]
    pair_devices = lax.axis_size("pair")
    per_owner = block_count // pair_devices
    capacity = max(2, (4 * row_count + 3 * block_count - 1) // (3 * block_count))
    freq_count = BANDS * NF
    owner_slots = per_owner * capacity
    lag_index = jnp.arange(lag_count, dtype=jnp.int32)
    live_rows = jnp.arange(row_count, dtype=jnp.int32) < pair_count[0]
    keep_mask = (
        (lag_index[None, :] >= lag_lo[:, None])
        & (lag_index[None, :] < lag_hi[:, None])
        & live_rows[:, None]
    )
    windowed = jnp.where(keep_mask[:, None, :], adjoint, jnp.zeros((), jnp.bfloat16))
    first_ids = first_block[:, 0]
    station_ids = jnp.arange(station_block.shape[0], dtype=jnp.int32)
    second_ids = jnp.sum(
        jnp.where(second_station[:, None] == station_ids[None, :], station_block[None, :], 0),
        axis=1,
    )
    members = (first_ids[:, None] == jnp.arange(block_count, dtype=jnp.int32)[None, :]).astype(
        jnp.int32
    )
    ranking = jnp.sum((jnp.cumsum(members, axis=0) - 1) * members, axis=1)
    destination = first_ids * capacity + ranking
    slot_ids = jnp.arange(block_count * capacity, dtype=jnp.int32)
    hits = slot_ids[:, None] == destination[None, :]
    dispatch = hits.astype(jnp.bfloat16)
    slot_second = jnp.sum(jnp.where(hits, second_ids[None, :], 0), axis=1)
    slot_second = slot_second.reshape(pair_devices, owner_slots)
    phase_table = dft_table(lag_count, freq_count, NF)
    packed = jnp.dot(dispatch, windowed.reshape(row_count, -1), preferred_element_type=jnp.float32)
    packed = packed.astype(jnp.bfloat16).reshape(pair_devices, owner_slots, comp_count, lag_count)
    arrived = transform_rows(
        lax.all_to_all(packed, "pair", split_axis=0, concat_axis=0, tiled=True), phase_table
    )
    arrived_second = lax.all_to_all(slot_second, "pair", split_axis=0, concat_axis=0, tiled=True)
    slot_block = jnp.arange(owner_slots, dtype=jnp.int32) // capacity
    pair_code = (slot_block[None, :] * block_count + arrived_second).reshape(-1)
    onehot = (
        pair_code[:, None] == jnp.arange(per_owner * block_count, dtype=jnp.int32)[None, :]
    ).astype(jnp.bfloat16)
    flat_spectra = arrived.reshape(pair_code.shape[0], -1)
    partial_value = jnp.einsum(
        "sk,sc->kc", onehot, flat_spectra, preferred_element_type=jnp.float32
    )
    summed = lax.psum(partial_value, "grid")
    coupling = summed.astype(jnp.bfloat16).reshape(
        per_owner, block_count, comp_count, 2, freq_count
    )
    spread = lax.all_to_all(coupling, "pair", split_axis=4, concat_axis=0, tiled=True)
    factors = spread.reshape(block_count, block_count, 3, 3, 2, local_freqs)
    coupling_re = factors[:, :, :, :, 0]
    coupling_im = factors[:, :, :, :, 1]
    green_re = green_function[:, :, 0]
    green_im = green_function[:, :, 1]
    response_re = contract(green_re, coupling_re) - contract(green_im, coupling_im)
    response_im = contract(green_re, coupling_im) + contract(green_im, coupling_re)
    density = jnp.sum(green_re * response_re + green_im * response_im, axis=(0, 1))
    first_freq = lax.axis_index("pair") * local_freqs
    freq_band = (first_freq + jnp.arange(local_freqs, dtype=jnp.int32)) // NF
    selector = freq_band[None, :] == jnp.arange(BANDS, dtype=jnp.int32)[:, None]
    kernel_part = jnp.sum(jnp.where(selector[:, :, None], density[None, :, :], 0.0), axis=1)
    return lax.psum(kernel_part, "pair")


def solution(mesh):
    placed = (
        P(("pair", "grid"), None, None),
        P(("pair", "grid"), None),
        P(("pair", "grid")),
        P(),
        P(("pair", "grid")),
        P(("pair", "grid")),
        P(("pair", "grid")),
        P(None, None, None, "pair", "grid"),
    )
    return jax.shard_map(
        body, mesh=mesh, in_specs=placed, out_specs=P(None, "grid"), check_vma=False
    )
```

profile of v0, /device:TPU:0, one launch (start us, length us, event | category | flops | bytes accessed | tf_op | source)
XLA Modules:
  0.0 472.7 jit_solution(14462065538232081586)
XLA Ops:
  0.0 0.7 fusion.31
  0.7 0.1 reduce_window_sum.11
  0.8 0.8 select_reduce_fusion.3
  1.7 0.7 multiply_add_fusion
  2.3 1.0 select_reduce_fusion
  3.3 0.1 select_reduce_fusion.2
  3.4 0.7 all_to_all.22
  4.1 7.3 %all-to-all-start = ((s32[8,1,12]{2,1,0:T(1,128)}), s32[8,1,12]{2,1,0:T(1,128)S(1)}, u32[]{:S(2)}, u32[]{:S(2)}) async-start(s32[8,1,12]{2,1,0:T(1,128)} %bitcast.2), calls=%async_computation | async-start | bytes 8192 | tf_op jit(solution)/shard_map/all_to_all | solution.py:74
  12.1 0.9 fusion.29
  13.0 2.0 broadcast_select_fusion
  14.9 3.4 copy.34
  18.4 6.3 %reshape.168 = bf16[64,18009]{1,0:T(8,128)(2,1)} reshape(bf16[64,9,2001]{2,1,0:T(8,128)(2,1)} %copy.34) | data formatting | bytes 4610304 | tf_op jit(solution)/shard_map/reshape | solution.py:69
  24.7 2.8 convolution_convert_fusion
  27.5 8.0 %reshape.169 = bf16[8,12,9,2001]{3,2,1,0:T(8,128)(2,1)} reshape(bf16[96,18009]{1,0:T(8,128)(2,1)S(1)} %convolution_convert_fusion) | data formatting | bytes 6915456 | tf_op jit(solution)/shard_map/reshape | solution.py:70
  35.5 7.7 %copy.35 = bf16[8,12,9,2001]{3,1,2,0:T(8,128)(2,1)} copy(bf16[8,12,9,2001]{3,2,1,0:T(8,128)(2,1)} %reshape.169) | data formatting | bytes 6915456 | tf_op jit(solution)/shard_map/reshape | solution.py:70
  43.2 0.0 all-to-all-done
  43.2 6.3 %all-to-all-start.1 = ((bf16[8,12,9,2001]{3,1,2,0:T(8,128)(2,1)}), bf16[8,12,9,2001]{3,1,2,0:T(8,128)(2,1)}, u32[]{:S(2)}, u32[]{:S(2)}) async-start(bf16[8,12,9,2001]{3,1,2,0:T(8,128)(2,1)} %copy.35), calls=%async_computation.1 | async-start | bytes 9437184 | tf_op jit(solution)/shard_map/all_to_all | solution.py:72
  49.5 0.1 add.97
  49.6 19.7 %cosine_convert_fusion = (bf16[2001,512]{1,0:T(8,128)(2,1)}, bf16[2001,512]{1,0:T(8,128)(2,1)}) fusion(s32[512]{0:T(512)S(1)} %fusion.35, s32[2001]{0:T(1024)S(1)} %iota_add_fusion), kind=kLoop, calls=%fused_computation.29 | loop fusion | flops 12294144 | bytes 4108100 | tf_op jit(solution)/shard_map/convert
  69.3 0.5 broadcast.196
  69.8 0.7 reduce.3
  70.5 0.1 all_to_all.24
  70.6 82.8 %all-to-all-done.1 = bf16[8,12,9,2001]{3,1,2,0:T(8,128)(2,1)} async-done(((bf16[8,12,9,2001]{3,1,2,0:T(8,128)(2,1)}), bf16[8,12,9,2001]{3,1,2,0:T(8,128)(2,1)}, u32[]{:S(2)}, u32[]{:S(2)}) %all-to-all-start.1) | async-done | bytes 3457760 | tf_op jit(solution)/shard_map/all_to_all | solution.py:72
  153.3 7.8 %copy.36 = bf16[8,12,9,2001]{3,2,1,0:T(8,128)(2,1)} copy(bf16[8,12,9,2001]{3,1,2,0:T(8,128)(2,1)} %all-to-all-done.1) | data formatting | bytes 6915456 | tf_op jit(solution)/shard_map/all_to_all | solution.py:72
  161.1 5.2 %reshape.170 = bf16[864,2001]{1,0:T(8,128)(2,1)S(1)} reshape(bf16[8,12,9,2001]{3,2,1,0:T(8,128)(2,1)} %copy.36) | data formatting | bytes 6915456 | tf_op jit(solution)/shard_map/reshape | solution.py:24
  166.4 7.2 %fusion.25 = bf16[864,1024]{1,0:T(8,128)(2,1)} fusion(bf16[864,2001]{1,0:T(8,128)(2,1)S(1)} %reshape.170, bf16[2001,512]{1,0:T(8,128)(2,1)} %get-tuple-element.8, bf16[2001,512]{1,0:T(8,128)(2,1)} %get-tuple-element.7), kind=kOutput, calls=%fused_computation.35 | convolution fusion | flops 3549794304 | bytes 9325248 | tf_op jit(solution)/shard_map/dot_general | solution.py:25
  173.6 3.9 reshape_reshape.3
  177.4 3.0 fusion.30
  180.5 84.7 %all-reduce.1 = bf16[128,9216]{1,0:T(8,128)(2,1)S(1)} all-reduce(f32[128,9216]{1,0:T(8,128)} %fusion.30), channel_id=1, replica_groups=mesh['pair'=8,'grid'=4] {'grid'}, use_global_device_ids=true, to_apply=%region_4.5 | all-reduce | flops 1179648 | bytes 7077888 | tf_op jit(solution)/shard_map/psum | solution.py:84
  265.1 2.9 reshape.171
  268.1 14.9 %copy.37 = bf16[4,32,9,2,512]{1,0,3,2,4:T(4,128)(2,1)} copy(bf16[4,32,9,2,512]{4,3,2,1,0:T(2,128)(2,1)} %reshape.171) | data formatting | bytes 4718592 | tf_op jit(solution)/shard_map/reshape | solution.py:85
  282.9 12.0 %reshape.188 = bf16[8,2,73728]{2,1,0:T(2,128)(2,1)} reshape(bf16[512,9,2,4,32]{4,3,2,1,0:T(4,128)(2,1)} %bitcast.74) | data formatting | bytes 4718592
  294.9 5.2 %all-to-all-start.2 = ((bf16[8,2,73728]{2,1,0:T(2,128)(2,1)}), bf16[8,2,73728]{2,1,0:T(2,128)(2,1)S(1)}, u32[]{:S(2)}, u32[]{:S(2)}) async-start(bf16[8,2,73728]{2,1,0:T(2,128)(2,1)} %reshape.188), calls=%async_computation.2 | async-start | bytes 4718592 | tf_op jit(solution)/shard_map/all_to_all | solution.py:88
  300.2 10.6 %fusion.41 = (bf16[32,3,1,64,512]{4,3,2,1,0:T(8,128)(2,1)}, bf16[32,3,1,64,512]{4,3,2,1,0:T(8,128)(2,1)}) fusion(bf16[32,3,2,64,512]{4,3,2,1,0:T(8,128)(2,1)} %param.15), kind=kLoop, calls=%fused_computation.76 | loop fusion | bytes 25165824 | tf_op jit(solution)/shard_map/slice | solution.py:92
  310.7 43.7 %all-to-all-done.2 = bf16[8,2,73728]{2,1,0:T(2,128)(2,1)S(1)} async-done(((bf16[8,2,73728]{2,1,0:T(2,128)(2,1)}), bf16[8,2,73728]{2,1,0:T(2,128)(2,1)S(1)}, u32[]{:S(2)}, u32[]{:S(2)}) %all-to-all-start.2) | async-done | bytes 2359328 | tf_op jit(solution)/shard_map/all_to_all | solution.py:88
  354.5 7.0 %reshape.189 = bf16[512,9,2,4,32]{4,3,2,1,0:T(4,128)(2,1)} reshape(bf16[8,2,73728]{2,1,0:T(2,128)(2,1)S(1)} %all-to-all-done.2) | data formatting | bytes 4718592
  361.5 0.0 slice-start
  361.5 0.0 slice-start.1
  361.5 7.1 %copy.38 = bf16[4,32,9,2,8,64]{1,0,4,2,5,3:T(4,128)(2,1)S(1)} copy(bf16[4,32,9,2,8,64]{1,0,3,2,5,4:T(4,128)(2,1)} %bitcast.75) | data formatting | bytes 4718592 | tf_op jit(solution)/shard_map/all_to_all | solution.py:88
  368.6 0.0 copy-start
  368.6 0.0 slice-done
  368.6 0.0 slice-done.1
  368.6 11.4 %fusion.6 = f32[64,32,3,512,1]{3,1,4,2,0:T(8,128)} fusion(bf16[32,3,1,64,512]{4,3,2,1,0:T(8,128)(2,1)S(1)} %bitcast.69, bf16[32,32,3,3,2,64]{1,0,3,2,5,4:T(8,128)(2,1)S(1)} %bitcast.70), kind=kOutput, calls=%fused_computation.11 | convolution fusion | flops 603979776 | bytes 23592960 | tf_op jit(solution)/shard_map/vbfx,uvabf->uafx/dot_general | solution.py:30
  380.0 11.9 %fusion.8 = f32[64,32,3,512,1]{3,1,4,2,0:T(8,128)} fusion(bf16[32,3,1,64,512]{4,3,2,1,0:T(8,128)(2,1)S(1)} %bitcast.69, bf16[32,32,3,3,2,64]{1,0,3,2,5,4:T(8,128)(2,1)S(1)} %bitcast.71), kind=kOutput, calls=%fused_computation.13 | convolution fusion | flops 603979776 | bytes 23592960 | tf_op jit(solution)/shard_map/vbfx,uvabf->uafx/dot_general | solution.py:30
  391.9 0.0 copy-done
  391.9 15.1 %fusion.2 = f32[64,32,3,512,1]{3,1,4,2,0:T(8,128)} fusion(bf16[32,3,1,64,512]{4,3,2,1,0:T(8,128)(2,1)} %get-tuple-element.6, bf16[32,32,3,3,2,64]{1,0,3,2,5,4:T(8,128)(2,1)S(1)} %bitcast.72), kind=kOutput, calls=%fused_computation.7 | convolution fusion | flops 603979776 | bytes 23592960 | tf_op jit(solution)/shard_map/vbfx,uvabf->uafx/dot_general | solution.py:30
  407.0 45.3 %fusion.1 = f32[64,512]{1,0:T(8,128)S(1)} fusion(f32[64,32,3,512,1]{3,1,4,2,0:T(8,128)} %fusion.2, f32[64,32,3,512,1]{3,1,4,2,0:T(8,128)} %fusion.6, f32[64,32,3,512,1]{3,1,4,2,0:T(8,128)} %fusion.8, bf16[32,3,1,64,512]{4,3,2,1,0:T(8,128)(2,1)} %get-tuple-element.6, bf16[32,3,1,64,512]{4,3,2,1,0:T(8,128)(2,1)} %get-tuple-element.5, ...), kind=kOutput, calls=%fused_computation.3 | convolution fusion | flops 629112832 | bytes 61472768 | tf_op jit(solution)/shard_map/vbfx,uvabf->uafx/dot_general | solution.py:30
  452.4 0.1 select_reduce_fusion.1
  452.5 20.1 %psum.15 = f32[2,512]{1,0:T(2,128)} all-reduce(f32[2,512]{1,0:T(2,128)S(1)} %select_reduce_fusion.1), channel_id=1, replica_groups=mesh['pair'=8,'grid'=4] {'pair'}, use_global_device_ids=true, to_apply=%region_7.8 | all-reduce | flops 1024 | bytes 8192 | tf_op jit(solution)/shard_map/psum | solution.py:101
  (9 shorter events, 0.1 us)
Async XLA Ops:
  4.1 39.1 %all-to-all-start = ((s32[8,1,12]{2,1,0:T(1,128)}), s32[8,1,12]{2,1,0:T(1,128)S(1)}, u32[]{:S(2)}, u32[]{:S(2)}) async-start(s32[8,1,12]{2,1,0:T(1,128)} %bitcast.2), calls=%async_computation | async-start | bytes 8192 | tf_op jit(solution)/shard_map/all_to_all | solution.py:74
  43.2 110.2 %all-to-all-start.1 = ((bf16[8,12,9,2001]{3,1,2,0:T(8,128)(2,1)}), bf16[8,12,9,2001]{3,1,2,0:T(8,128)(2,1)}, u32[]{:S(2)}, u32[]{:S(2)}) async-start(bf16[8,12,9,2001]{3,1,2,0:T(8,128)(2,1)} %copy.35), calls=%async_computation.1 | async-start | bytes 9437184 | tf_op jit(solution)/shard_map/all_to_all | solution.py:72
  294.9 59.5 %all-to-all-start.2 = ((bf16[8,2,73728]{2,1,0:T(2,128)(2,1)}), bf16[8,2,73728]{2,1,0:T(2,128)(2,1)S(1)}, u32[]{:S(2)}, u32[]{:S(2)}) async-start(bf16[8,2,73728]{2,1,0:T(2,128)(2,1)} %reshape.188), calls=%async_computation.2 | async-start | bytes 4718592 | tf_op jit(solution)/shard_map/all_to_all | solution.py:88
  361.5 7.2 %slice-start = ((s8[6291456]{0:T(1024)(128)(4,1)}), s8[4194304]{0:T(1024)(128)(4,1)S(1)}, s32[]{:S(2)}) async-start(s8[6291456]{0:T(1024)(128)(4,1)} %bitcast.68), calls=%async_computation.3 | async-start | bytes 8388608
  361.5 7.2 %slice-start.1 = ((s8[6291456]{0:T(1024)(128)(4,1)}), s8[2097152]{0:T(1024)(128)(4,1)S(1)}, s32[]{:S(2)}) async-start(s8[6291456]{0:T(1024)(128)(4,1)} %bitcast.68), calls=%async_computation.4 | async-start | bytes 4194304
  368.6 23.3 %copy-start = (bf16[4,32,9,2,8,64]{1,0,4,2,5,3:T(4,128)(2,1)}, bf16[4,32,9,2,8,64]{1,0,4,2,5,3:T(4,128)(2,1)S(1)}, u32[]{:S(2)}) copy-start(bf16[4,32,9,2,8,64]{1,0,4,2,5,3:T(4,128)(2,1)S(1)} %copy.38) | copy-start | bytes 7077892
where the time goes:
time: 480 us; the launch traced here: 473 us
  waiting for transfers between devices  127 us (26%)
  blocking collectives  105 us (22%)
  local copies, waits for them, and re-layouts  98.2 us (20%)
  matrix products  96.7 us (20%)
  other arithmetic  26.8 us (6%)
  starting transfers between devices  18.8 us (4%)
    psum x1, blocking collectives, body(): summed = lax.psum(partial_value, 'grid')  84.7 us
    dot_general x4, matrix products, contract(): jnp.einsum('vbfx,uvabf->uafx', field, factor, preferred_element_type=jnp....  83.7 us
    all_to_all x1, waiting for transfers between devices, body(): lax.all_to_all(packed, 'pair', split_axis=0, concat_axis=0, tiled=True)  82.8 us
    all_to_all x1, waiting for transfers between devices, body(): lax.all_to_all(coupling, 'pair', split_axis=4, concat_axis=0, tiled=True)  43.7 us
    psum x1, blocking collectives, body(): return lax.psum(kernel_part, 'pair')  20.1 us
    another operation x1, other arithmetic  19.7 us
    unnamed x8, local copies, waits for them, and re-layouts  19 us
    reshape x2, local copies, waits for them, and re-layouts, body(): summed.astype(jnp.bfloat16)  17.8 us
  transfers between devices with their start and end apart: 3, of which 2 were waited for; matrix products, arithmetic and copies ran while one was open for 13% of the time, Pallas kernels for 0%

commit v1 on v0

--- a/solution.py
+++ b/solution.py
@@ -1,8 +1,11 @@
+import functools
 import math
 
 import jax
 import jax.numpy as jnp
 from jax import lax
+from jax.experimental import pallas as pl
+from jax.experimental.pallas import tpu as pltpu
 from jax.sharding import PartitionSpec as P
 
 NF = 256
@@ -101,6 +104,251 @@
     return lax.psum(kernel_part, "pair")
 
 
+STEP = 32
+PAD_ROWS = 16
+
+
+def twiddles(lag_count, freq_count, band_width, owners):
+    per_owner = freq_count // owners
+    column = jnp.arange(2 * freq_count, dtype=jnp.int32)[None, :]
+    quarter = (column // per_owner) % 2
+    index = (column // (2 * per_owner)) * per_owner + column % per_owner
+    freq_bin = 24 + index + 64 * (index // band_width)
+    coarse_count = -(-lag_count // STEP)
+    coarse = STEP * jnp.arange(coarse_count, dtype=jnp.int32)[:, None] - lag_count // 2
+    fine = jnp.arange(STEP, dtype=jnp.int32)[:, None]
+    turn = 2.0 * math.pi / lag_count
+    coarse_phase = jnp.mod(coarse * freq_bin, lag_count).astype(jnp.float32) * turn
+    coarse_phase = coarse_phase + quarter.astype(jnp.float32) * (0.5 * math.pi)
+    fine_phase = jnp.mod(fine * freq_bin, lag_count).astype(jnp.float32) * turn
+    return jnp.cos(coarse_phase), jnp.sin(coarse_phase), jnp.cos(fine_phase), jnp.sin(fine_phase)
+
+
+def spectra_kernel(
+    owners, lo_ref, hi_ref, count_ref, adjoint_ref, ca_ref, sa_ref, cb_ref, sb_ref, out_ref, win, table, spec
+):
+    rows, comps, lags = adjoint_ref.shape
+    padded = win.shape[1]
+    width = table.shape[1] // owners
+    coarse = ca_ref.shape[0]
+    tail = (lags // 128) * 128
+    win[:, tail:] = jnp.zeros((win.shape[0], padded - tail), jnp.bfloat16)
+    table[coarse * STEP :, :] = jnp.zeros((padded - coarse * STEP, table.shape[1]), jnp.bfloat16)
+    for i in range(coarse):
+        part = ca_ref[i : i + 1, :] * cb_ref[...] - sa_ref[i : i + 1, :] * sb_ref[...]
+        table[i * STEP : (i + 1) * STEP, :] = part.astype(jnp.bfloat16)
+    lag = lax.broadcasted_iota(jnp.int32, (comps, lags), 1)
+    zero_rows = jnp.zeros((PAD_ROWS - comps, padded), jnp.bfloat16)
+    live = count_ref[0]
+
+    def window(p, carry):
+        low = lo_ref[p]
+        high = jnp.where(p < live, hi_ref[p], 0)
+        keep = (lag >= low) & (lag < high)
+        kept = jnp.where(keep, adjoint_ref[p].astype(jnp.float32), 0.0).astype(jnp.bfloat16)
+        start = pl.multiple_of(p * PAD_ROWS, PAD_ROWS)
+        win[pl.ds(start, PAD_ROWS), :lags] = jnp.concatenate([kept, zero_rows[:, :lags]], axis=0)
+        return carry
+
+    lax.fori_loop(0, rows, window, 0, unroll=4)
+    chunk = 2 * width
+    for n in range(table.shape[1] // chunk):
+        part = jnp.dot(win[...], table[:, n * chunk : (n + 1) * chunk], preferred_element_type=jnp.float32)
+        spec[:, n * chunk : (n + 1) * chunk] = part.astype(jnp.bfloat16)
+    for c in range(comps):
+        target = lax.broadcasted_iota(jnp.int32, (rows, rows * PAD_ROWS), 0) * PAD_ROWS + c
+        source = lax.broadcasted_iota(jnp.int32, (rows, rows * PAD_ROWS), 1)
+        select = (target == source).astype(jnp.float32).astype(jnp.bfloat16)
+        picked = jnp.dot(select, spec[...], preferred_element_type=jnp.float32).astype(jnp.bfloat16)
+        for o in range(owners):
+            out_ref[o, :, c * width : (c + 1) * width] = picked[:, o * width : (o + 1) * width]
+
+
+def spectra_of(adjoint, lag_lo, lag_hi, pair_count, owners):
+    rows, comps, lags = adjoint.shape
+    tables = twiddles(lags, BANDS * NF, NF, owners)
+    padded = -(-lags // 128) * 128
+    columns = 2 * BANDS * NF
+    smem = pl.BlockSpec(memory_space=pltpu.SMEM)
+    vmem = pl.BlockSpec(memory_space=pltpu.VMEM)
+    return pl.pallas_call(
+        functools.partial(spectra_kernel, owners),
+        out_shape=jax.ShapeDtypeStruct((owners, rows, comps * (columns // owners)), jnp.bfloat16),
+        in_specs=[smem, smem, smem] + [vmem] * 5,
+        out_specs=vmem,
+        scratch_shapes=[
+            pltpu.VMEM((rows * PAD_ROWS, padded), jnp.bfloat16),
+            pltpu.VMEM((padded, columns), jnp.bfloat16),
+            pltpu.VMEM((rows * PAD_ROWS, columns), jnp.bfloat16),
+        ],
+        compiler_params=pltpu.CompilerParams(vmem_limit_bytes=48 * 1024 * 1024),
+        name="spectra",
+    )(lag_lo, lag_hi, pair_count, adjoint, *tables)
+
+
+def swap_matrix(n):
+    r = lax.broadcasted_iota(jnp.int32, (n * n, n * n), 0)
+    s = lax.broadcasted_iota(jnp.int32, (n * n, n * n), 1)
+    same = (r // n == s % n) & (r % n == s // n)
+    return same.astype(jnp.float32).astype(jnp.bfloat16)
+
+
+def transpose_green(green_ref, raw, turned, sems, fetch_only=False, start=0):
+    pass
+
+
+def green_copy(green_ref, raw, sems, part):
+    return pltpu.make_async_copy(
+        green_ref.at[:, :, :, pl.ds(part * 16, 16), :], raw.at[part % 2], sems.at[part % 2]
+    )
+
+
+def turn_green(green_ref, raw, turned, sems):
+    swap = swap_matrix(16)
+    blocks = green_ref.shape[0]
+    freqs, points = green_ref.shape[3], green_ref.shape[4]
+    parts = freqs // 16
+    for ri in range(2):
+        turned[:, 128 * ri + 3 * blocks : 128 * (ri + 1), :] = jnp.zeros(
+            (freqs, 128 - 3 * blocks, points), jnp.bfloat16
+        )
+    for part in range(parts):
+        green_copy(green_ref, raw, sems, part).wait()
+        slot = part % 2
+        for ri in range(2):
+            for b in range(3):
+                for v in range(0, blocks, 16):
+                    block = raw[slot, v : v + 16, b, ri].reshape(256, points)
+                    moved = jnp.dot(swap, block, preferred_element_type=jnp.float32)
+                    row = 128 * ri + b * blocks + v
+                    turned[part * 16 : (part + 1) * 16, row : row + 16, :] = (
+                        moved.astype(jnp.bfloat16).reshape(16, 16, points)
+                    )
+        if part + 2 < parts:
+            green_copy(green_ref, raw, sems, part + 2).start()
+
+
+def couple(code_of, value_ref, blocks, by_lane):
+    pairs = value_ref.shape[0]
+    eye = (
+        lax.broadcasted_iota(jnp.int32, (128, 128), 0) == lax.broadcasted_iota(jnp.int32, (128, 128), 1)
+    ).astype(jnp.float32).astype(jnp.bfloat16)
+    codes = code_of()
+    group = 8
+    gap = jnp.zeros((128 - 3 * blocks, 128), jnp.bfloat16)
+
+    def some(i, carry):
+        cell = lax.broadcasted_iota(jnp.int32, (group * blocks, pairs), 0) + i * (group * blocks)
+        onehot = (cell == codes).astype(jnp.float32).astype(jnp.bfloat16)
+        sums = jnp.dot(onehot, value_ref[...], preferred_element_type=jnp.float32).astype(jnp.bfloat16)
+        for u in range(group):
+            rows = sums[u * blocks : (u + 1) * blocks]
+            pieces = []
+            for a in range(3):
+                for b in range(3):
+                    c = 3 * a + b
+                    pieces.append(rows[:, c * 128 : (c + 1) * 128])
+                pieces.append(gap)
+            stacked = jnp.concatenate(pieces, axis=0)
+            flipped = lax.dot_general(
+                eye, stacked, (((1,), (1,)), ((), ())), preferred_element_type=jnp.float32
+            ).astype(jnp.bfloat16)
+            for a in range(3):
+                by_lane[a * blocks + i * group + u] = flipped[:, a * 128 : (a + 1) * 128]
+        return carry
+
+    lax.fori_loop(0, blocks // group, some, 0)
+
+
+def spread_matrix(by_lane, system):
+    swap = swap_matrix(16)
+    count = by_lane.shape[0]
+    freqs = system.shape[0]
+    for ri in range(2):
+        for f in range(0, freqs, 16):
+            for i in range(0, count, 16):
+                block = by_lane[i : i + 16, ri * freqs + f : ri * freqs + f + 16, :].reshape(256, 128)
+                moved = jnp.dot(swap, block, preferred_element_type=jnp.float32)
+                moved = moved.reshape(16, 16, 128)
+                value = moved.astype(jnp.bfloat16)
+                if ri == 0:
+                    system[f : f + 16, i : i + 16, 0:128] = value
+                    system[f : f + 16, count + i : count + i + 16, 128:256] = value
+                else:
+                    system[f : f + 16, count + i : count + i + 16, 0:128] = value
+                    system[f : f + 16, i : i + 16, 128:256] = (-moved).astype(jnp.bfloat16)
+
+
+def quadratic(system, turned):
+    freqs, rows, _ = system.shape
+    points = turned.shape[2]
+    half = rows // 2
+
+    def one(f, total):
+        field = turned[f]
+        response = jnp.dot(system[f], field, preferred_element_type=jnp.float32)
+        product = (
+            response[:half] * field[:half].astype(jnp.float32)
+            + response[half:] * field[128 : 128 + half].astype(jnp.float32)
+        )
+        return total + jnp.sum(product.reshape(half // 8, 8, points), axis=0)
+
+    total = lax.fori_loop(0, freqs, one, jnp.zeros((8, points), jnp.float32), unroll=2)
+    return jnp.sum(total, axis=0, keepdims=True)
+
+
+def density_kernel(code_ref, value_ref, green_ref, out_ref, raw, turned, by_lane, system, sems):
+    blocks = green_ref.shape[0]
+    for part in range(2):
+        green_copy(green_ref, raw, sems, part).start()
+    turn_green(green_ref, raw, turned, sems)
+    couple(lambda: code_ref[...], value_ref, blocks, by_lane)
+    spread_matrix(by_lane, system)
+    out_ref[...] = quadratic(system, turned)
+
+
+def density_of(codes, values, green):
+    blocks, _, _, freqs, points = green.shape
+    vmem = pl.BlockSpec(memory_space=pltpu.VMEM)
+    return pl.pallas_call(
+        density_kernel,
+        out_shape=jax.ShapeDtypeStruct((1, points), jnp.float32),
+        in_specs=[vmem, vmem, pl.BlockSpec(memory_space=pl.ANY)],
+        out_specs=vmem,
+        scratch_shapes=[
+            pltpu.VMEM((2, blocks, 3, 2, 16, points), jnp.bfloat16),
+            pltpu.VMEM((freqs, 256, points), jnp.bfloat16),
+            pltpu.VMEM((3 * blocks, 128, 128), jnp.bfloat16),
+            pltpu.VMEM((freqs, 6 * blocks, 256), jnp.bfloat16),
+            pltpu.SemaphoreType.DMA((2,)),
+        ],
+        compiler_params=pltpu.CompilerParams(vmem_limit_bytes=56 * 1024 * 1024),
+        name="density",
+    )(codes, values, green)
+
+
+def fast_body(
+    adjoint, first_block, second_station, station_block, lag_lo, lag_hi, pair_count, green_function
+):
+    blocks = green_function.shape[0]
+    owners = lax.axis_size("pair")
+    local_freqs = green_function.shape[3]
+    station_ids = jnp.arange(station_block.shape[0], dtype=jnp.int32)
+    second_ids = jnp.sum(
+        jnp.where(second_station[:, None] == station_ids[None, :], station_block[None, :], 0), axis=1
+    )
+    codes = first_block[:, 0] * blocks + second_ids
+    codes = lax.all_gather(codes, ("grid", "pair"), tiled=True)[None, :]
+    spectra = spectra_of(adjoint, lag_lo, lag_hi, pair_count, owners)
+    arrived = lax.all_to_all(spectra, "pair", split_axis=0, concat_axis=0, tiled=True)
+    arrived = arrived.reshape(-1, arrived.shape[-1])
+    values = lax.all_gather(arrived, "grid", tiled=True)
+    density = density_of(codes, values, green_function)
+    band = lax.axis_index("pair") * local_freqs // NF
+    selector = jnp.arange(BANDS, dtype=jnp.int32)[:, None] == band
+    return lax.psum(jnp.where(selector, density, 0.0), "pair")
+
+
 def solution(mesh):
     placed = (
         P(("pair", "grid"), None, None),
@@ -112,6 +360,7 @@
         P(("pair", "grid")),
         P(None, None, None, "pair", "grid"),
     )
+    local_freqs = BANDS * NF // mesh.shape["pair"]
     return jax.shard_map(
-        body, mesh=mesh, in_specs=placed, out_specs=P(None, "grid"), check_vma=False
-    )
+        fast_body if local_freqs == 64 else body, mesh=mesh, in_specs=placed, out_specs=P(None, "grid"), check_vma=False
+    )

time: 480 us -> 159 us (0.33); the launches traced: 473 us -> 158 us
  waiting for transfers between devices: 127 us -> 0.03 us
  matrix products: 96.7 us -> 0 us
  local copies, waits for them, and re-layouts: 98.2 us -> 3.78 us
  Pallas kernels: 0 us -> 39.9 us
  other arithmetic: 26.8 us -> 2.93 us
  starting transfers between devices: 18.8 us -> 0.01 us
  between operations: 1.04 us -> 14.9 us
  blocking collectives: 105 us -> 96.5 us
    all_to_all x3 -> x0, waiting for transfers between devices: 127 us -> none  [the longest x1 82.8 us: body(): lax.all_to_all(packed, 'pair', split_axis=0, concat_axis=0, tiled=True)]
    dot_general x7 -> x0, matrix products: 96.7 us -> none  [the longest x4 83.7 us: contract(): jnp.einsum('vbfx,uvabf->uafx', field, factor, preferred_element_type=jnp....]
    psum x2 -> x1, blocking collectives: 105 us -> 21.3 us  [fast_body(): return lax.psum(jnp.where(selector, density, 0.0), 'pair')]
    reshape x6 -> x0, local copies, waits for them, and re-layouts: 45 us -> none  [the longest x2 17.8 us: body(): summed.astype(jnp.bfloat16)]
    pallas_call x0 -> x2, Pallas kernels: none -> 39.9 us  [the longest x1 28.4 us: density_of(): pl.pallas_call(density_kernel, out_shape=jax.ShapeDtypeStruct((1, points)...]
    unnamed x0 -> x1, blocking collectives: none -> 39.1 us
    all_to_all x0 -> x1, blocking collectives: none -> 36.1 us  [fast_body(): lax.all_to_all(spectra, 'pair', split_axis=0, concat_axis=0, tiled=True)]
    another operation x2 -> x0, other arithmetic: 19.8 us -> none
  transfers between devices with their start and end apart: 3 -> 1, of which waited for: 2 -> 0; matrix products, arithmetic and copies ran while one was open for 13% -> 1% of each run, Pallas kernels for 0% -> 0%
where the time goes in v1:
time: 159 us; the launch traced here: 158 us
  blocking collectives  96.5 us (61%)
  Pallas kernels  39.9 us (25%)
  between operations  14.9 us (9%)
  local copies, waits for them, and re-layouts  3.78 us (2%)
  other arithmetic  2.93 us (2%)
    unnamed x1, blocking collectives  39.1 us
    all_to_all x1, blocking collectives, fast_body(): lax.all_to_all(spectra, 'pair', split_axis=0, concat_axis=0, tiled=True)  36.1 us
    pallas_call x1, Pallas kernels, density_of(): pl.pallas_call(density_kernel, out_shape=jax.ShapeDtypeStruct((1, points)...  28.4 us
    psum x1, blocking collectives, fast_body(): return lax.psum(jnp.where(selector, density, 0.0), 'pair')  21.3 us
    pallas_call x1, Pallas kernels, spectra_of(): pl.pallas_call(functools.partial(spectra_kernel, owners), out_shape=jax.S...  11.5 us
    unnamed x15, local copies, waits for them, and re-layouts  3.78 us
  transfers between devices with their start and end apart: 1, of which 0 were waited for; matrix products, arithmetic and copies ran while one was open for 1% of the time, Pallas kernels for 0%

profile of v1, /device:TPU:0, one launch (start us, length us, event | category | flops | bytes accessed | tf_op | source)
XLA Modules:
  0.0 158.1 jit_solution(14952411241910035145)
XLA Ops:
  6.5 0.0 copy-start
  6.5 0.0 copy-start.1
  6.5 0.0 all-gather.2.cloned.1.call-start
  6.6 0.6 fusion.12
  7.1 3.2 %copy.10.adjoint_ref = bf16[64,9,2001]{2,1,0:T(8,128)(2,1)S(1)} copy(bf16[64,9,2001]{2,0,1:T(8,128)(2,1)} %param.8) | data formatting | bytes 4610304 | tf_op args[0]
  11.0 1.2 fusion.5
  12.1 0.0 copy-done
  12.1 0.0 copy-done.1
  12.2 0.0 copy-start.5
  12.2 0.0 copy-start.2
  12.2 0.0 copy-start.3
  12.2 0.0 copy-start.4
  12.2 11.5 %spectra.1 = bf16[8,64,1152]{2,1,0:T(8,128)(2,1)S(1)} custom-call(s32[64]{0:T(128)S(1)} %copy-done, s32[64]{0:T(128)S(1)} %copy-done.1, s32[1]{0:T(128)S(6)} %copy.12.count_ref, bf16[64,9,2001]{2,1,0:T(8,128)(2,1)S(1)} %copy.10.adjoint_ref, f32[63,1024]{1,0:T(8,128)S(1)} %get-tuple-element.6.ca_ref, f32[63,1024]{1,0:T(8,128)S(1)} %get-tuple-element.5.sa_ref, ...), custom_call_target="tpu_custom_call" | custom-call | tf_op jit(solution)/shard_map/spectra/pallas_call | solution.py:174
  23.7 36.1 %all_to_all.5 = bf16[8,64,1152]{2,1,0:T(8,128)(2,1)} all-to-all(bf16[8,64,1152]{2,1,0:T(8,128)(2,1)S(1)} %spectra.1), channel_id=1, replica_groups=mesh['pair'=8,'grid'=4] {'pair'}, dimensions={0} | all-to-all | bytes 2359296 | tf_op jit(solution)/shard_map/all_to_all | solution.py:343
  59.8 0.0 all-gather.2.cloned.1.call-update
  59.9 0.0 copy-done.5
  59.9 0.6 dynamic-slice
  61.1 0.0 copy-done.2
  61.1 0.0 copy-done.3
  61.1 0.3 select_reduce_fusion
  61.4 0.0 copy-done.4
  61.4 0.1 fusion.33
  61.6 39.1 %all-reduce = s32[2048]{0:T(1024)} all-reduce(s32[2048]{0:T(1024)S(1)} %fusion.33), channel_id=1, replica_groups=mesh['pair'=8,'grid'=4] {'grid','pair'}, use_global_device_ids=true, to_apply=%add | all-reduce | flops 2048 | bytes 16384
  100.6 0.0 all-gather.2.cloned.1.call-done.value_ref
  100.7 28.4 %density.1 = f32[1,512]{1,0:T(1,128)} custom-call(s32[1,2048]{1,0:T(1,128)} %bitcast.9, bf16[2048,1152]{1,0:T(8,128)(2,1)} %all-gather.2.cloned.1.call-done.value_ref, bf16[32,3,2,64,512]{4,3,2,1,0:T(8,128)(2,1)} %green_ref.1), custom_call_target="tpu_custom_call" | custom-call | tf_op jit(solution)/shard_map/density/pallas_call | solution.py:313
  129.1 0.8 broadcast_select_fusion
  129.9 21.3 %psum.7 = f32[2,512]{1,0:T(2,128)} all-reduce(f32[2,512]{1,0:T(2,128)S(1)} %broadcast_select_fusion), channel_id=1, replica_groups=mesh['pair'=8,'grid'=4] {'pair'}, use_global_device_ids=true, to_apply=%region_1.2 | all-reduce | flops 1024 | bytes 8192 | tf_op jit(solution)/shard_map/psum | solution.py:349
  (5 shorter events, 0.0 us)
Async XLA Ops:
  6.5 5.6 %copy-start = (s32[64]{0:T(128)S(1)}, s32[64]{0:T(128)}, u32[]{:S(2)}) copy-start(s32[64]{0:T(128)} %lo_ref.1) | copy-start | bytes 772
  6.5 5.6 %copy-start.1 = (s32[64]{0:T(128)S(1)}, s32[64]{0:T(128)}, u32[]{:S(2)}) copy-start(s32[64]{0:T(128)} %hi_ref.1) | copy-start | bytes 772
  6.5 94.1 %all-gather.2.cloned.1.call-start = ((), (), s32[]{:S(2)}) async-start(), calls=%async_computation.1 | async-start | bytes 5898240 | tf_op jit(solution)/shard_map/all_gather | solution.py:345
  12.2 47.7 %copy-start.5 = (u32[32]{0:T(128)S(1)}, u32[32]{0:T(128)}, u32[]{:S(2)}) copy-start(u32[32]{0:T(128)} %constant.117) | copy-start | bytes 388
  12.2 48.9 %copy-start.2 = (s32[4000]{0:T(1024)S(1)}, s32[4000]{0:T(1024)}, u32[]{:S(2)}) copy-start(s32[4000]{0:T(1024)} %param.11) | copy-start | bytes 48004
  12.2 48.9 %copy-start.3 = (s32[64]{0:T(128)S(1)}, s32[64]{0:T(128)}, u32[]{:S(2)}) copy-start(s32[64]{0:T(128)} %param.10) | copy-start | bytes 772
  12.2 49.2 %copy-start.4 = (s32[64,1]{0,1:T(1,128)S(1)}, s32[64,1]{0,1:T(1,128)}, u32[]{:S(2)}) copy-start(s32[64,1]{0,1:T(1,128)} %param.9) | copy-start | bytes 772
Sparse Core Ops, SparseCore 0:
  60.0 36.4 all-gather.1

commit v2 on v0

--- a/solution.py
+++ b/solution.py
@@ -1,8 +1,11 @@
+import functools
 import math
 
 import jax
 import jax.numpy as jnp
 from jax import lax
+from jax.experimental import pallas as pl
+from jax.experimental.pallas import tpu as pltpu
 from jax.sharding import PartitionSpec as P
 
 NF = 256
@@ -101,6 +104,387 @@
     return lax.psum(kernel_part, "pair")
 
 
+STEP = 32
+
+
+def twiddles(lag_count, freq_count, band_width, owners):
+    per_owner = freq_count // owners
+    column = jnp.arange(2 * freq_count, dtype=jnp.int32)[None, :]
+    quarter = (column // per_owner) % 2
+    index = (column // (2 * per_owner)) * per_owner + column % per_owner
+    freq_bin = 24 + index + 64 * (index // band_width)
+    coarse_count = -(-lag_count // STEP)
+    coarse = STEP * jnp.arange(coarse_count, dtype=jnp.int32)[:, None] - lag_count // 2
+    fine = jnp.arange(STEP, dtype=jnp.int32)[:, None]
+    turn = 2.0 * math.pi / lag_count
+    coarse_phase = jnp.mod(coarse * freq_bin, lag_count).astype(jnp.float32) * turn
+    coarse_phase = coarse_phase + quarter.astype(jnp.float32) * (0.5 * math.pi)
+    fine_phase = jnp.mod(fine * freq_bin, lag_count).astype(jnp.float32) * turn
+    return jnp.cos(coarse_phase), jnp.sin(coarse_phase), jnp.cos(fine_phase), jnp.sin(fine_phase)
+
+
+def swap_matrix(n):
+    r = lax.broadcasted_iota(jnp.int32, (n * n, n * n), 0)
+    s = lax.broadcasted_iota(jnp.int32, (n * n, n * n), 1)
+    same = (r // n == s % n) & (r % n == s // n)
+    return same.astype(jnp.float32).astype(jnp.bfloat16)
+
+
+def green_copy(green_ref, raw, sems, part):
+    return pltpu.make_async_copy(
+        green_ref.at[:, :, :, pl.ds(part * 16, 16), :], raw.at[part % 2], sems.at[part % 2]
+    )
+
+
+def clear_gaps(turned, blocks):
+    freqs, _, points = turned.shape
+    for ri in range(2):
+        turned[:, 128 * ri + 3 * blocks : 128 * (ri + 1), :] = jnp.zeros(
+            (freqs, 128 - 3 * blocks, points), jnp.bfloat16
+        )
+
+
+def turn_green(green_ref, raw, turned, sems, swap, part, ri):
+    blocks, points = green_ref.shape[0], green_ref.shape[4]
+    slot = part % 2
+    if ri == 0:
+        green_copy(green_ref, raw, sems, part).wait()
+    for b in range(3):
+        for v in range(0, blocks, 16):
+            block = raw[slot, v : v + 16, b, ri].reshape(256, points)
+            moved = jnp.dot(swap, block, preferred_element_type=jnp.float32)
+            row = 128 * ri + b * blocks + v
+            turned[part * 16 : (part + 1) * 16, row : row + 16, :] = (
+                moved.astype(jnp.bfloat16).reshape(16, 16, points)
+            )
+    if ri == 1 and part + 2 < green_ref.shape[3] // 16:
+        green_copy(green_ref, raw, sems, part + 2).start()
+
+
+def couple(codes, value_ref, blocks, by_lane):
+    pairs = value_ref.shape[0] * value_ref.shape[1]
+    eye = (
+        lax.broadcasted_iota(jnp.int32, (128, 128), 0) == lax.broadcasted_iota(jnp.int32, (128, 128), 1)
+    ).astype(jnp.float32).astype(jnp.bfloat16)
+    group = 8
+    gap = jnp.zeros((128 - 3 * blocks, 128), jnp.bfloat16)
+
+    def some(i, carry):
+        cell = lax.broadcasted_iota(jnp.int32, (group * blocks, pairs), 0) + i * (group * blocks)
+        onehot = (cell == codes).astype(jnp.float32).astype(jnp.bfloat16)
+        values = value_ref[...].reshape(pairs, value_ref.shape[2])
+        sums = jnp.dot(onehot, values, preferred_element_type=jnp.float32).astype(jnp.bfloat16)
+        for u in range(group):
+            rows = sums[u * blocks : (u + 1) * blocks]
+            pieces = []
+            for a in range(3):
+                for b in range(3):
+                    c = 3 * a + b
+                    pieces.append(rows[:, c * 128 : (c + 1) * 128])
+                pieces.append(gap)
+            stacked = jnp.concatenate(pieces, axis=0)
+            flipped = lax.dot_general(
+                eye, stacked, (((1,), (1,)), ((), ())), preferred_element_type=jnp.float32
+            ).astype(jnp.bfloat16)
+            for a in range(3):
+                by_lane[a * blocks + i * group + u] = flipped[:, a * 128 : (a + 1) * 128]
+        return carry
+
+    lax.fori_loop(0, blocks // group, some, 0)
+
+
+def spread_matrix(by_lane, system):
+    swap = swap_matrix(16)
+    count = by_lane.shape[0]
+    freqs = system.shape[0]
+    for ri in range(2):
+        for f in range(0, freqs, 16):
+            for i in range(0, count, 16):
+                block = by_lane[i : i + 16, ri * freqs + f : ri * freqs + f + 16, :].reshape(256, 128)
+                moved = jnp.dot(swap, block, preferred_element_type=jnp.float32)
+                moved = moved.reshape(16, 16, 128)
+                value = moved.astype(jnp.bfloat16)
+                if ri == 0:
+                    system[f : f + 16, i : i + 16, 0:128] = value
+                    system[f : f + 16, count + i : count + i + 16, 128:256] = value
+                else:
+                    system[f : f + 16, count + i : count + i + 16, 0:128] = value
+                    system[f : f + 16, i : i + 16, 128:256] = (-moved).astype(jnp.bfloat16)
+
+
+def quadratic(system, turned):
+    freqs, rows, _ = system.shape
+    points = turned.shape[2]
+    half = rows // 2
+
+    def one(f, total):
+        field = turned[f]
+        response = jnp.dot(system[f], field, preferred_element_type=jnp.float32)
+        product = (
+            response[:half] * field[:half].astype(jnp.float32)
+            + response[half:] * field[128 : 128 + half].astype(jnp.float32)
+        )
+        return total + jnp.sum(product.reshape(half // 8, 8, points), axis=0)
+
+    total = lax.fori_loop(0, freqs, one, jnp.zeros((8, points), jnp.float32), unroll=2)
+    return jnp.sum(total, axis=0, keepdims=True)
+
+
+def make_table(table, ca_ref, sa_ref, cb_ref, sb_ref):
+    coarse = ca_ref.shape[0]
+    table[coarse * STEP :, :] = jnp.zeros((table.shape[0] - coarse * STEP, table.shape[1]), jnp.bfloat16)
+    for i in range(coarse):
+        part = ca_ref[i : i + 1, :] * cb_ref[...] - sa_ref[i : i + 1, :] * sb_ref[...]
+        table[i * STEP : (i + 1) * STEP, :] = part.astype(jnp.bfloat16)
+
+
+def make_window(win, adjoint_ref, lo_ref, hi_ref):
+    comps, rows, lags = adjoint_ref.shape
+    tail = (lags // 128) * 128
+    win[:, tail:] = jnp.zeros((win.shape[0], win.shape[1] - tail), jnp.bfloat16)
+    lag = lax.broadcasted_iota(jnp.int32, (rows, lags), 1)
+    keep = (lag >= lo_ref[...]) & (lag < hi_ref[...])
+    for c in range(comps):
+        kept = jnp.where(keep, adjoint_ref[c].astype(jnp.float32), 0.0)
+        win[c * rows : (c + 1) * rows, :lags] = kept.astype(jnp.bfloat16)
+
+
+def main_kernel(
+    owners,
+    adjoint_ref,
+    lo_ref,
+    hi_ref,
+    code_ref,
+    ca_ref,
+    sa_ref,
+    cb_ref,
+    sb_ref,
+    green_ref,
+    out_ref,
+    win,
+    table,
+    outbox,
+    values,
+    codes,
+    raw,
+    turned,
+    by_lane,
+    system,
+    parts,
+    green_sems,
+    own_sems,
+    send_pair,
+    recv_pair,
+    send_chip,
+    recv_chip,
+    send_core,
+    recv_core,
+    send_part,
+    recv_part,
+):
+    comps, rows, _ = adjoint_ref.shape
+    blocks, freqs = green_ref.shape[0], green_ref.shape[3]
+    pair, grid = lax.axis_index("pair"), lax.axis_index("grid")
+    other_chip = lax.rem(grid + 2, 4)
+    other_core = grid + 1 - 2 * lax.rem(grid, 2)
+    barrier = pltpu.get_barrier_semaphore()
+
+    def greet(p, g):
+        pl.semaphore_signal(barrier, inc=1, device_id=(p, g), device_id_type=pl.DeviceIdType.MESH)
+
+    for k in range(1, owners):
+        greet(lax.rem(pair + k, owners), grid)
+    greet(pair, other_chip)
+    greet(pair, other_core)
+    for part in range(2):
+        green_copy(green_ref, raw, green_sems, part).start()
+    make_table(table, ca_ref, sa_ref, cb_ref, sb_ref)
+    make_window(win, adjoint_ref, lo_ref, hi_ref)
+    pl.semaphore_wait(barrier, owners + 1)
+
+    width = 2 * freqs
+    couples = owners // 2
+    z, y = pair // 2, lax.rem(pair, 2)
+    mine = grid * owners + pair
+
+    def remote(src, dst, send, recv, p, g):
+        return pltpu.make_async_remote_copy(
+            src_ref=src, dst_ref=dst, send_sem=send, recv_sem=recv,
+            device_id=(p, g), device_id_type=pl.DeviceIdType.MESH,
+        )
+
+    def to_owner(o):
+        return (
+            remote(outbox.at[o], values.at[mine], send_pair.at[0, o], recv_pair.at[0, pair], o, grid),
+            remote(code_ref, codes.at[mine], send_pair.at[1, o], recv_pair.at[1, pair], o, grid),
+        )
+
+    def from_source(q):
+        slot = grid * owners + q
+        return (
+            remote(outbox.at[q], values.at[slot], send_pair.at[0, q], recv_pair.at[0, q], q, grid),
+            remote(code_ref, codes.at[slot], send_pair.at[1, q], recv_pair.at[1, q], q, grid),
+        )
+
+    def between_chips(q, from_grid):
+        slot = from_grid * owners + q
+        return tuple(
+            remote(ref.at[slot], ref.at[slot], send_chip.at[i, q], recv_chip.at[i, q], pair, other_chip)
+            for i, ref in enumerate((values, codes))
+        )
+
+    def between_cores(q, from_grid, turn):
+        slot = from_grid * owners + q
+        return tuple(
+            remote(
+                ref.at[slot], ref.at[slot], send_core.at[i, turn, q], recv_core.at[i, turn, q],
+                pair, other_core,
+            )
+            for i, ref in enumerate((values, codes))
+        )
+
+    order = [0] + [couples // 2] + [k for k in range(1, couples) if k != couples // 2]
+    for k in order:
+        zz = lax.rem(z + k, couples)
+        start = pl.multiple_of(zz * 2 * width, 2 * width)
+        spectra = jnp.dot(
+            win[...], table[:, pl.ds(start, 2 * width)], preferred_element_type=jnp.float32
+        ).astype(jnp.bfloat16)
+        for h in range(2):
+            for c in range(comps):
+                outbox[2 * zz + h, :, c * width : (c + 1) * width] = spectra[
+                    c * rows : (c + 1) * rows, h * width : (h + 1) * width
+                ]
+        if k == 0:
+            own = (
+                pltpu.make_async_copy(outbox.at[pair], values.at[mine], own_sems.at[0]),
+                pltpu.make_async_copy(code_ref, codes.at[mine], own_sems.at[1]),
+            )
+            for copy in own:
+                copy.start()
+            for copy in to_owner(2 * z + 1 - y):
+                copy.start()
+            for copy in own:
+                copy.wait()
+            for copy in between_chips(pair, grid) + between_cores(pair, grid, 0):
+                copy.start()
+        else:
+            for h in range(2):
+                for copy in to_owner(2 * zz + h):
+                    copy.start()
+
+    sources = [pair, 2 * z + 1 - y]
+    for k in order[1:]:
+        back = lax.rem(z + couples - k, couples)
+        sources += [2 * back, 2 * back + 1]
+    swap = swap_matrix(16)
+    clear_gaps(turned, blocks)
+    green_steps = [(part, ri) for part in range(freqs // 16) for ri in range(2)]
+    for step, q in enumerate(sources):
+        turn_green(green_ref, raw, turned, green_sems, swap, *green_steps[step])
+        if step > 0:
+            for copy in from_source(q):
+                copy.wait_recv()
+            for copy in between_chips(q, grid) + between_cores(q, grid, 0):
+                copy.start()
+            before = sources[step - 1]
+            for copy in between_chips(before, grid):
+                copy.wait_recv()
+            for copy in between_cores(before, other_chip, 1):
+                copy.start()
+    last = sources[-1]
+    for copy in between_chips(last, grid):
+        copy.wait_recv()
+    for copy in between_cores(last, other_chip, 1):
+        copy.start()
+    for q in sources:
+        for copy in between_cores(q, grid, 0) + between_cores(q, other_chip, 1):
+            copy.wait_recv()
+
+    code_row = jnp.concatenate([codes[i][0:1, 0:rows] for i in range(codes.shape[0])], axis=1)
+    couple(code_row, values, blocks, by_lane)
+    spread_matrix(by_lane, system)
+    parts[pair] = quadratic(system, turned)
+
+    def to_peer(k):
+        there = lax.rem(pair + k, owners)
+        return remote(parts.at[pair], parts.at[pair], send_part.at[there], recv_part.at[pair], there, grid)
+
+    def from_peer(k):
+        there = lax.rem(pair + k, owners)
+        return remote(parts.at[there], parts.at[there], send_part.at[there], recv_part.at[there], there, grid)
+
+    for k in range(1, owners):
+        to_peer(k).start()
+    for k in range(1, owners):
+        from_peer(k).wait_recv()
+    for band in range(BANDS):
+        members = [parts[o] for o in range(owners) if o * freqs // NF == band]
+        out_ref[band : band + 1, :] = sum(members[1:], members[0])
+    for q in sources:
+        for copy in between_chips(q, grid) + between_cores(q, grid, 0) + between_cores(q, other_chip, 1):
+            copy.wait_send()
+    for q in sources[1:]:
+        for copy in to_owner(q):
+            copy.wait_send()
+    for k in range(1, owners):
+        to_peer(k).wait_send()
+
+
+def fast_body(
+    adjoint, first_block, second_station, station_block, lag_lo, lag_hi, pair_count, green_function
+):
+    rows, comps, lags = adjoint.shape
+    blocks, _, _, freqs, points = green_function.shape
+    owners, grids = lax.axis_size("pair"), lax.axis_size("grid")
+    station_ids = jnp.arange(station_block.shape[0], dtype=jnp.int32)
+    second_ids = jnp.sum(
+        jnp.where(second_station[:, None] == station_ids[None, :], station_block[None, :], 0), axis=1
+    )
+    code = first_block[:, 0] * blocks + second_ids
+    code = jnp.broadcast_to(jnp.pad(code, (0, 128 - rows))[None, :], (8, 128))
+    live = jnp.arange(rows, dtype=jnp.int32) < pair_count[0]
+    high = jnp.where(live, lag_hi, 0)[:, None]
+    tables = twiddles(lags, BANDS * NF, NF, owners)
+    padded = -(-lags // 128) * 128
+    columns = 2 * BANDS * NF
+    chunks = owners * grids
+    vmem = pl.BlockSpec(memory_space=pltpu.VMEM)
+    dma = pltpu.SemaphoreType.DMA
+    return pl.pallas_call(
+        functools.partial(main_kernel, owners),
+        out_shape=jax.ShapeDtypeStruct((BANDS, points), jnp.float32),
+        in_specs=[vmem] * 8 + [pl.BlockSpec(memory_space=pl.ANY)],
+        out_specs=vmem,
+        scratch_shapes=[
+            pltpu.VMEM((rows * comps, padded), jnp.bfloat16),
+            pltpu.VMEM((padded, columns), jnp.bfloat16),
+            pltpu.VMEM((owners, rows, comps * 2 * freqs), jnp.bfloat16),
+            pltpu.VMEM((chunks, rows, comps * 2 * freqs), jnp.bfloat16),
+            pltpu.VMEM((chunks, 8, 128), jnp.int32),
+            pltpu.VMEM((2, blocks, 3, 2, 16, points), jnp.bfloat16),
+            pltpu.VMEM((freqs, 256, points), jnp.bfloat16),
+            pltpu.VMEM((3 * blocks, 128, 128), jnp.bfloat16),
+            pltpu.VMEM((freqs, 6 * blocks, 256), jnp.bfloat16),
+            pltpu.VMEM((owners, 1, points), jnp.float32),
+            dma((2,)),
+            dma((2,)),
+            dma((2, owners)),
+            dma((2, owners)),
+            dma((2, owners)),
+            dma((2, owners)),
+            dma((2, 2, owners)),
+            dma((2, 2, owners)),
+            dma((owners,)),
+            dma((owners,)),
+        ],
+        compiler_params=pltpu.CompilerParams(
+            collective_id=0, has_side_effects=True, vmem_limit_bytes=60 * 1024 * 1024
+        ),
+        name="sensitivity",
+    )(jnp.transpose(adjoint, (1, 0, 2)), lag_lo[:, None], high, code, *tables, green_function)
+
+
 def solution(mesh):
     placed = (
         P(("pair", "grid"), None, None),
@@ -112,6 +496,7 @@
         P(("pair", "grid")),
         P(None, None, None, "pair", "grid"),
     )
+    local_freqs = BANDS * NF // mesh.shape["pair"]
     return jax.shard_map(
-        body, mesh=mesh, in_specs=placed, out_specs=P(None, "grid"), check_vma=False
-    )
+        fast_body if local_freqs == 64 else body, mesh=mesh, in_specs=placed, out_specs=P(None, "grid"), check_vma=False
+    )

time: 480 us -> 87.7 us (0.18); the launches traced: 473 us -> 87.4 us
  waiting for transfers between devices: 127 us -> 0 us
  blocking collectives: 105 us -> 0 us
  matrix products: 96.7 us -> 0 us
  local copies, waits for them, and re-layouts: 98.2 us -> 3.91 us
  Pallas kernels: 0 us -> 77.2 us
  other arithmetic: 26.8 us -> 5.61 us
  starting transfers between devices: 18.8 us -> 0 us
    all_to_all x3 -> x0, waiting for transfers between devices: 127 us -> none  [the longest x1 82.8 us: body(): lax.all_to_all(packed, 'pair', split_axis=0, concat_axis=0, tiled=True)]
    psum x2 -> x0, blocking collectives: 105 us -> none  [the longest x1 84.7 us: body(): summed = lax.psum(partial_value, 'grid')]
    dot_general x7 -> x0, matrix products: 96.7 us -> none  [the longest x4 83.7 us: contract(): jnp.einsum('vbfx,uvabf->uafx', field, factor, preferred_element_type=jnp....]
    pallas_call x0 -> x1, Pallas kernels: none -> 77.2 us  [fast_body(): pl.pallas_call(functools.partial(main_kernel, owners), out_shape=jax.Shap...]
    reshape x6 -> x0, local copies, waits for them, and re-layouts: 45 us -> none  [the longest x2 17.8 us: body(): summed.astype(jnp.bfloat16)]
    another operation x2 -> x0, other arithmetic: 19.8 us -> none
    all_to_all x3 -> x0, starting transfers between devices: 18.8 us -> none  [the longest x1 7.28 us: body(): lax.all_to_all(slot_second, 'pair', split_axis=0, concat_axis=0, tiled=True)]
    unnamed x8 -> x1, local copies, waits for them, and re-layouts: 19 us -> 1.27 us
  transfers between devices with their start and end apart: 3 -> 0, of which waited for: 2 -> 0; matrix products, arithmetic and copies ran while one was open for 13% -> 0% of each run, Pallas kernels for 0% -> 0%
where the time goes in v2:
time: 87.7 us; the launch traced here: 87.4 us
  Pallas kernels  77.2 us (88%)
  other arithmetic  5.61 us (6%)
  local copies, waits for them, and re-layouts  3.91 us (4%)
    pallas_call x1, Pallas kernels, fast_body(): pl.pallas_call(functools.partial(main_kernel, owners), out_shape=jax.Shap...  77.2 us
    sin x1, other arithmetic, twiddles(): jnp.sin(coarse_phase)  2.01 us

profile of v2, /device:TPU:0, one launch (start us, length us, event | category | flops | bytes accessed | tf_op | source)
XLA Modules:
  0.0 87.4 jit_solution(4860111151880922749)
XLA Ops:
  0.0 2.0 %fusion.5 = (f32[63,1024]{1,0:T(8,128)}, f32[63,1024]{1,0:T(8,128)}) fusion(f32[1024]{0:T(1024)S(1)} %fusion.28, s32[1024]{0:T(1024)S(1)} %fusion.25, s32[63]{0:T(128)S(1)} %multiply_add_fusion), kind=kLoop, calls=%fused_computation.9 | loop fusion | flops 645120 | bytes 524540 | tf_op jit(solution)/shard_map/sin | solution.py:123
  2.0 1.3 %fusion.12 = (f32[32,1024]{1,0:T(8,128)}, f32[32,1024]{1,0:T(8,128)}) fusion(s32[1024]{0:T(1024)S(1)} %fusion.25), kind=kLoop, calls=%fused_computation.18 | loop fusion | flops 294912 | bytes 266240 | tf_op jit(solution)/shard_map/sin | solution.py:123
  4.0 0.7 fusion.33
  4.6 0.7 copy.12.hi_ref
  5.3 1.3 %copy.11.lo_ref = s32[64,1]{1,0:T(8,128)} copy(s32[64,1]{0,1:T(1,128)} %bitcast.9) | data formatting | bytes 512 | tf_op jit(solution)/shard_map/broadcast_in_dim | solution.py:485
  6.7 1.0 %select_reduce_fusion = s32[64]{0:T(128)S(1)} fusion(s32[4000]{0:T(1024)} %param.11, s32[64]{0:T(128)} %param.10), kind=kLoop, calls=%fused_computation | loop fusion | flops 767936 | bytes 16512 | tf_op jit(solution)/shard_map/reduce_sum | solution.py:441
  7.6 0.7 bitcast_add_fusion
  8.3 0.6 broadcast_in_dim.39.code_ref
  8.9 77.2 %sensitivity.1 = f32[2,512]{1,0:T(2,128)} custom-call(bf16[9,64,2001]{2,1,0:T(8,128)(2,1)} %bitcast.8, s32[64,1]{1,0:T(8,128)} %copy.11.lo_ref, s32[64,1]{1,0:T(8,128)} %copy.12.hi_ref, s32[8,128]{1,0:T(8,128)} %broadcast_in_dim.39.code_ref, f32[63,1024]{1,0:T(8,128)} %get-tuple-element.6.ca_ref, f32[63,1024]{1,0:T(8,128)} %get-tuple-element.5.sa_ref, ...), custom_call_target="tpu_custom_call" | custom-call | tf_op jit(solution)/shard_map/sensitivity/pallas_call | solution.py:454
  86.1 1.3 %copy.15 = f32[2,512]{1,0:T(2,128)} copy(f32[2,512]{1,0:T(2,128)} %sensitivity.1) | data formatting | bytes 8192
  (4 shorter events, 0.0 us)

commit v3 on v2

--- a/solution.py
+++ b/solution.py
@@ -113,14 +113,13 @@
     quarter = (column // per_owner) % 2
     index = (column // (2 * per_owner)) * per_owner + column % per_owner
     freq_bin = 24 + index + 64 * (index // band_width)
-    coarse_count = -(-lag_count // STEP)
-    coarse = STEP * jnp.arange(coarse_count, dtype=jnp.int32)[:, None] - lag_count // 2
-    fine = jnp.arange(STEP, dtype=jnp.int32)[:, None]
-    turn = 2.0 * math.pi / lag_count
-    coarse_phase = jnp.mod(coarse * freq_bin, lag_count).astype(jnp.float32) * turn
-    coarse_phase = coarse_phase + quarter.astype(jnp.float32) * (0.5 * math.pi)
-    fine_phase = jnp.mod(fine * freq_bin, lag_count).astype(jnp.float32) * turn
-    return jnp.cos(coarse_phase), jnp.sin(coarse_phase), jnp.cos(fine_phase), jnp.sin(fine_phase)
+    row = jnp.arange(16 + STEP, dtype=jnp.int32)[:, None]
+    offset = jnp.where(
+        row < 8, 8 * STEP * row - lag_count // 2, jnp.where(row < 16, STEP * (row - 8), row - 16)
+    )
+    phase = jnp.mod(offset * freq_bin, lag_count).astype(jnp.float32) * (2.0 * math.pi / lag_count)
+    phase = phase + jnp.where(row < 8, quarter, 0).astype(jnp.float32) * (0.5 * math.pi)
+    return jnp.cos(phase), jnp.sin(phase)
 
 
 def swap_matrix(n):
@@ -226,24 +225,54 @@
         )
         return total + jnp.sum(product.reshape(half // 8, 8, points), axis=0)
 
-    total = lax.fori_loop(0, freqs, one, jnp.zeros((8, points), jnp.float32), unroll=2)
+    total = lax.fori_loop(0, freqs, one, jnp.zeros((8, points), jnp.float32), unroll=4)
     return jnp.sum(total, axis=0, keepdims=True)
 
 
-def make_table(table, ca_ref, sa_ref, cb_ref, sb_ref):
-    coarse = ca_ref.shape[0]
-    table[coarse * STEP :, :] = jnp.zeros((table.shape[0] - coarse * STEP, table.shape[1]), jnp.bfloat16)
-    for i in range(coarse):
-        part = ca_ref[i : i + 1, :] * cb_ref[...] - sa_ref[i : i + 1, :] * sb_ref[...]
-        table[i * STEP : (i + 1) * STEP, :] = part.astype(jnp.bfloat16)
-
-
-def make_window(win, adjoint_ref, lo_ref, hi_ref):
+def make_table(table, cos_ref, sin_ref):
+    cos_mid, sin_mid = cos_ref[8:16, :], sin_ref[8:16, :]
+    cos_fine, sin_fine = cos_ref[16:, :], sin_ref[16:, :]
+    for i in range(table.shape[0] // (8 * STEP)):
+        cos_top, sin_top = cos_ref[i : i + 1, :], sin_ref[i : i + 1, :]
+        cos_part = cos_top * cos_mid - sin_top * sin_mid
+        sin_part = sin_top * cos_mid + cos_top * sin_mid
+        for j in range(8):
+            part = cos_part[j : j + 1] * cos_fine - sin_part[j : j + 1] * sin_fine
+            row = (8 * i + j) * STEP
+            table[row : row + STEP, :] = part.astype(jnp.bfloat16)
+
+
+def to_column(row):
+    n = row.shape[1]
+    same = lax.broadcasted_iota(jnp.int32, (n, n), 0) == lax.broadcasted_iota(jnp.int32, (n, n), 1)
+    return jnp.sum(jnp.where(same, row.astype(jnp.float32), 0.0), axis=1, keepdims=True)
+
+
+def to_row(column):
+    n = column.shape[0]
+    same = lax.broadcasted_iota(jnp.int32, (n, n), 0) == lax.broadcasted_iota(jnp.int32, (n, n), 1)
+    return jnp.sum(jnp.where(same, column, 0.0), axis=0, keepdims=True)
+
+
+def make_codes(code_ref, first_ref, second_ref, station_ref, blocks):
+    rows, stations = first_ref.shape[1], station_ref.shape[1]
+    second = to_column(second_ref[...]).astype(jnp.int32)
+    hit = lax.broadcasted_iota(jnp.int32, (rows, stations), 1) == second
+    named = jnp.where(hit, station_ref[...].astype(jnp.float32), 0.0)
+    named = to_row(jnp.sum(named, axis=1, keepdims=True)).astype(jnp.int32)
+    code_ref[...] = jnp.zeros(code_ref.shape, jnp.int32)
+    code_ref[0:1, 0:rows] = first_ref[...] * blocks + named
+
+
+def make_window(win, adjoint_ref, lo_ref, hi_ref, count_ref):
     comps, rows, lags = adjoint_ref.shape
+    live = lax.broadcasted_iota(jnp.int32, (1, rows), 1) < count_ref[...]
+    low = to_column(lo_ref[...]).astype(jnp.int32)
+    high = to_column(jnp.where(live, hi_ref[...], 0)).astype(jnp.int32)
     tail = (lags // 128) * 128
     win[:, tail:] = jnp.zeros((win.shape[0], win.shape[1] - tail), jnp.bfloat16)
     lag = lax.broadcasted_iota(jnp.int32, (rows, lags), 1)
-    keep = (lag >= lo_ref[...]) & (lag < hi_ref[...])
+    keep = (lag >= low) & (lag < high)
     for c in range(comps):
         kept = jnp.where(keep, adjoint_ref[c].astype(jnp.float32), 0.0)
         win[c * rows : (c + 1) * rows, :lags] = kept.astype(jnp.bfloat16)
@@ -254,15 +283,17 @@
     adjoint_ref,
     lo_ref,
     hi_ref,
-    code_ref,
-    ca_ref,
-    sa_ref,
-    cb_ref,
-    sb_ref,
+    count_ref,
+    first_ref,
+    second_ref,
+    station_ref,
+    cos_ref,
+    sin_ref,
     green_ref,
     out_ref,
     win,
     table,
+    code_ref,
     outbox,
     values,
     codes,
@@ -298,8 +329,9 @@
     greet(pair, other_core)
     for part in range(2):
         green_copy(green_ref, raw, green_sems, part).start()
-    make_table(table, ca_ref, sa_ref, cb_ref, sb_ref)
-    make_window(win, adjoint_ref, lo_ref, hi_ref)
+    make_codes(code_ref, first_ref, second_ref, station_ref, blocks)
+    make_table(table, cos_ref, sin_ref)
+    make_window(win, adjoint_ref, lo_ref, hi_ref, count_ref)
     pl.semaphore_wait(barrier, owners + 1)
 
     width = 2 * freqs
@@ -343,7 +375,7 @@
             for i, ref in enumerate((values, codes))
         )
 
-    order = [0] + [couples // 2] + [k for k in range(1, couples) if k != couples // 2]
+    order = [0] + [k for k in range(1, couples) if k != couples // 2] + [couples // 2]
     for k in order:
         zz = lax.rem(z + k, couples)
         start = pl.multiple_of(zz * 2 * width, 2 * width)
@@ -373,6 +405,12 @@
                 for copy in to_owner(2 * zz + h):
                     copy.start()
 
+    def pass_on(q):
+        for copy in between_chips(q, grid):
+            copy.wait_recv()
+        for copy in between_cores(q, other_chip, 1):
+            copy.start()
+
     sources = [pair, 2 * z + 1 - y]
     for k in order[1:]:
         back = lax.rem(z + couples - k, couples)
@@ -387,16 +425,10 @@
                 copy.wait_recv()
             for copy in between_chips(q, grid) + between_cores(q, grid, 0):
                 copy.start()
-            before = sources[step - 1]
-            for copy in between_chips(before, grid):
-                copy.wait_recv()
-            for copy in between_cores(before, other_chip, 1):
-                copy.start()
-    last = sources[-1]
-    for copy in between_chips(last, grid):
-        copy.wait_recv()
-    for copy in between_cores(last, other_chip, 1):
-        copy.start()
+        if step >= 2:
+            pass_on(sources[step - 2])
+    for q in sources[len(sources) - 2 :]:
+        pass_on(q)
     for q in sources:
         for copy in between_cores(q, grid, 0) + between_cores(q, other_chip, 1):
             copy.wait_recv()
@@ -437,16 +469,8 @@
     rows, comps, lags = adjoint.shape
     blocks, _, _, freqs, points = green_function.shape
     owners, grids = lax.axis_size("pair"), lax.axis_size("grid")
-    station_ids = jnp.arange(station_block.shape[0], dtype=jnp.int32)
-    second_ids = jnp.sum(
-        jnp.where(second_station[:, None] == station_ids[None, :], station_block[None, :], 0), axis=1
-    )
-    code = first_block[:, 0] * blocks + second_ids
-    code = jnp.broadcast_to(jnp.pad(code, (0, 128 - rows))[None, :], (8, 128))
-    live = jnp.arange(rows, dtype=jnp.int32) < pair_count[0]
-    high = jnp.where(live, lag_hi, 0)[:, None]
     tables = twiddles(lags, BANDS * NF, NF, owners)
-    padded = -(-lags // 128) * 128
+    padded = -(-lags // (8 * STEP)) * (8 * STEP)
     columns = 2 * BANDS * NF
     chunks = owners * grids
     vmem = pl.BlockSpec(memory_space=pltpu.VMEM)
@@ -454,11 +478,12 @@
     return pl.pallas_call(
         functools.partial(main_kernel, owners),
         out_shape=jax.ShapeDtypeStruct((BANDS, points), jnp.float32),
-        in_specs=[vmem] * 8 + [pl.BlockSpec(memory_space=pl.ANY)],
+        in_specs=[vmem] * 9 + [pl.BlockSpec(memory_space=pl.ANY)],
         out_specs=vmem,
         scratch_shapes=[
             pltpu.VMEM((rows * comps, padded), jnp.bfloat16),
             pltpu.VMEM((padded, columns), jnp.bfloat16),
+            pltpu.VMEM((8, 128), jnp.int32),
             pltpu.VMEM((owners, rows, comps * 2 * freqs), jnp.bfloat16),
             pltpu.VMEM((chunks, rows, comps * 2 * freqs), jnp.bfloat16),
             pltpu.VMEM((chunks, 8, 128), jnp.int32),
@@ -482,7 +507,17 @@
             collective_id=0, has_side_effects=True, vmem_limit_bytes=60 * 1024 * 1024
         ),
         name="sensitivity",
-    )(jnp.transpose(adjoint, (1, 0, 2)), lag_lo[:, None], high, code, *tables, green_function)
+    )(
+        jnp.transpose(adjoint, (1, 0, 2)),
+        lag_lo[None, :],
+        lag_hi[None, :],
+        pair_count[None, :],
+        first_block.reshape(1, rows),
+        second_station[None, :],
+        station_block[None, :],
+        *tables,
+        green_function,
+    )
 
 
 def solution(mesh):

time: 87.7 us -> 73.9 us (0.84)
  Pallas kernels: 77.2 us -> 70 us
  other arithmetic: 5.61 us -> 1.69 us
  local copies, waits for them, and re-layouts: 3.91 us -> 1.28 us
    pallas_call x1, Pallas kernels: 77.2 us -> 70 us  [fast_body(): pl.pallas_call(functools.partial(main_kernel, owners), out_shape=jax.Shap...]
    broadcast_in_dim x3 -> x0, local copies, waits for them, and re-layouts: 2.63 us -> none  [the longest x1 1.34 us: fast_body(): lag_lo[:, None]]
    sin x2 -> x1, other arithmetic: 3.27 us -> 1.66 us  [twiddles(): return (jnp.cos(phase), jnp.sin(phase))]
    reduce_sum x1 -> x0, other arithmetic: 0.99 us -> none  [fast_body(): jnp.sum(jnp.where(second_station[:, None] == station_ids[None, :], statio...]
where the time goes in v3:
time: 73.9 us; the launch traced here: 73.7 us
  Pallas kernels  70 us (95%)
  other arithmetic  1.69 us (2%)
  local copies, waits for them, and re-layouts  1.28 us (2%)
    pallas_call x1, Pallas kernels, fast_body(): pl.pallas_call(functools.partial(main_kernel, owners), out_shape=jax.Shap...  70 us
    sin x1, other arithmetic, twiddles(): return (jnp.cos(phase), jnp.sin(phase))  1.66 us

profile of v3, /device:TPU:0, one launch (start us, length us, event | category | flops | bytes accessed | tf_op | source)
XLA Modules:
  0.0 73.7 jit_solution(192330230669138341)
XLA Ops:
  0.0 1.7 %fusion.6 = (f32[48,1024]{1,0:T(8,128)}, f32[48,1024]{1,0:T(8,128)}) fusion(s32[1024]{0:T(1024)S(1)} %get-tuple-element.7, s32[1024]{0:T(1024)S(1)} %get-tuple-element.8, s32[48]{0:T(128)S(1)} %fusion.25, pred[48]{0:T(512)(128)(4,1)S(1)} %iota_compare_fusion), kind=kLoop, calls=%fused_computation.8 | loop fusion | flops 638976 | bytes 401648 | tf_op jit(solution)/shard_map/sin | solution.py:122
  2.4 70.0 %sensitivity.1 = f32[2,512]{1,0:T(2,128)} custom-call(bf16[9,64,2001]{2,1,0:T(8,128)(2,1)} %bitcast.8, s32[1,64]{1,0:T(1,128)} %bitcast.10, s32[1,64]{1,0:T(1,128)} %bitcast.11, s32[1,1]{1,0:T(1,128)} %bitcast.7.count_ref, s32[1,64]{1,0:T(1,128)} %bitcast.12, s32[1,64]{1,0:T(1,128)} %bitcast.13, s32[1,4000]{1,0:T(1,128)} %bitcast.9, ...), custom_call_target="tpu_custom_call" | custom-call | tf_op jit(solution)/shard_map/sensitivity/pallas_call | solution.py:478
  72.4 1.3 %copy.11 = f32[2,512]{1,0:T(2,128)} copy(f32[2,512]{1,0:T(2,128)} %sensitivity.1) | data formatting | bytes 8192
  (3 shorter events, 0.0 us)
